TPU v7x, 32 devices: a whole 2x2x4 slice. The times are simulated.
32 devices in a mesh: od: 16 (over z, x, core), lk: 2 (over y).
Axes of the slice: x: 2, y: 2, z: 4, core: 2. Of those that a mesh axis runs over, the one named last changes fastest.
Arguments:
- factor: bfloat16 [131072, 256], P('od'), may hold values from -6 to 6
- prior_mean: bfloat16 [131072], P('od'), may hold values from -192 to 192
- counts: float32 [16384], P(('od', 'lk')), may hold values from -8192 to 8192
- noise_std: float32 [16384], P(('od', 'lk')), may hold values from 1638.4 to 16384
- owner_ids: int32 [128, 8], P('od'), may hold values from 0 to 15, all different within a row; in each aligned block of 8 rows (0 to 7, 8 to 15, ...) at most 8 rows name the same one
- local_ids: int32 [128, 8], P('od'), may hold values from 0 to 63
- ecmp: int32 [128, 8], P('od'), may hold values from 1 to 4
- route_share: bfloat16 [128, 8, 128, 128], P('od'), may hold values from 0 to 1
Outputs:
- new_factor: float32 [131072, 256], P(('od', 'lk'))
- correction: float32 [131072], P(('od', 'lk'))
Inputs may be any that keep to these rules, and one draw needn't show every extreme that they name: `owner_ids`: each tile names 8 different owners; the 8 tiles of one aligned group name any owner at most 8 times, and some group names some owner exactly 8 times.
All inputs are finite; a program needn't handle non-finite values.
Results may differ from a plain program's by a relative error of at most 0.0003.
Values may be sent and summed in bfloat16 or wider, within the bound.
A program may use at most 128 MiB of HBM per device.

v0:
```python
import jax
import jax.numpy as jnp
from jax import lax
from jax.sharding import PartitionSpec as P


def slot_numbers(owners_flat):
    entries = owners_flat.shape[-1]
    matching = owners_flat[..., :, None] == owners_flat[..., None, :]
    earlier = lax.broadcasted_iota(jnp.int32, (entries, entries), 1) < lax.broadcasted_iota(
        jnp.int32, (entries, entries), 0
    )
    return jnp.sum((matching & earlier).astype(jnp.int32), axis=-1)


def requests_for(owner_part, local_part, slot_cap):
    owners_count = lax.axis_size("od")
    owner_flat = owner_part.reshape(-1)
    local_flat = local_part.reshape(-1)
    own_slots = slot_numbers(owner_flat)
    owner_iota = lax.broadcasted_iota(jnp.int32, (owners_count, slot_cap, 1), 0)
    slot_iota = lax.broadcasted_iota(jnp.int32, (owners_count, slot_cap, 1), 1)
    wanted = (owner_flat[None, None, :] == owner_iota) & (own_slots[None, None, :] == slot_iota)
    asking = jnp.sum(jnp.where(wanted, local_flat[None, None, :], 0), axis=-1)
    incoming = lax.all_to_all(asking, "od", split_axis=0, concat_axis=0, tiled=True)
    return (incoming, owner_flat, own_slots)


def per_device(factor, prior_mean, counts, noise_std, owner_ids, local_ids, ecmp, route_share):
    tiles_here, blocks_tile = owner_ids.shape
    link_dev = counts.shape[0]
    rank_full = factor.shape[1]
    block_rows = route_share.shape[3]
    owners_count = lax.axis_size("od")
    lk_count = lax.axis_size("lk")
    lk_index = lax.axis_index("lk")
    slot_cap = min(tiles_here, max(2, 2 * tiles_here * blocks_tile // owners_count))
    fac_rows = factor.reshape(-1, block_rows, rank_full)
    mean_rows = prior_mean.reshape(-1, block_rows)
    incoming, owner_flat, own_slots = requests_for(owner_ids, local_ids, slot_cap)
    multiples = ecmp.astype(jnp.float32)
    position = owner_flat * slot_cap + own_slots
    cols = rank_full // lk_count
    picked = lax.dynamic_slice_in_dim(fac_rows[incoming], lk_index * cols, cols, 3)
    sent_factor = jnp.swapaxes(picked, 2, 3)
    sent_mean = mean_rows[incoming]
    got_factor, got_mean = (
        lax.all_to_all(sent_factor, "od", split_axis=0, concat_axis=0, tiled=True),
        lax.all_to_all(sent_mean, "od", split_axis=0, concat_axis=0, tiled=True),
    )
    tile_factor = got_factor.reshape(-1, cols, block_rows)[position].reshape(
        tiles_here, blocks_tile, cols, block_rows
    )
    tile_mean = got_mean.reshape(-1, block_rows)[position].reshape(
        tiles_here, blocks_tile, block_rows
    )
    products = jnp.einsum(
        "tkab,tkcb->tkca", route_share, tile_factor, preferred_element_type=jnp.float32
    )
    summed = jnp.sum(products * multiples[:, :, None, None], axis=1)
    linked_part = jnp.transpose(summed, (1, 0, 2)).reshape(cols, -1)
    linked_t = lax.all_to_all(linked_part, "lk", split_axis=1, concat_axis=0, tiled=True)
    mean_terms = jnp.einsum(
        "tkab,tkb->tka", route_share, tile_mean, preferred_element_type=jnp.float32
    )
    predicted = jnp.sum(mean_terms * multiples[:, :, None], axis=1).reshape(-1)
    predicted_own = lax.dynamic_slice_in_dim(predicted, lk_index * link_dev, link_dev)
    whitened_t = linked_t / noise_std[None, :]
    innovation = (counts - predicted_own) / noise_std
    gram_local = jnp.dot(
        whitened_t,
        whitened_t.T,
        precision=lax.Precision.HIGHEST,
        preferred_element_type=jnp.float32,
    )
    projected_local = jnp.dot(
        whitened_t, innovation, precision=lax.Precision.HIGHEST, preferred_element_type=jnp.float32
    )
    gram, projected = lax.psum((gram_local, projected_local), ("od", "lk"))
    identity = jnp.eye(gram.shape[0], dtype=jnp.float32)
    lower = jnp.linalg.cholesky(identity + gram)
    inverse = jax.scipy.linalg.solve_triangular(lower, identity, lower=True)
    inner = jnp.dot(
        inverse, projected, precision=lax.Precision.HIGHEST, preferred_element_type=jnp.float32
    )
    gain_vector = jnp.dot(
        inverse.T, inner, precision=lax.Precision.HIGHEST, preferred_element_type=jnp.float32
    )
    row_share = factor.shape[0] // lk_count
    own_rows = lax.dynamic_slice_in_dim(factor, lk_index * row_share, row_share, 0).astype(
        jnp.float32
    )
    new_factor = jnp.dot(
        own_rows, inverse.T, precision=lax.Precision.HIGHEST, preferred_element_type=jnp.float32
    )
    correction = jnp.dot(
        own_rows, gain_vector, precision=lax.Precision.HIGHEST, preferred_element_type=jnp.float32
    )
    return (new_factor, correction)


def solution(mesh):
    in_specs = (
        P("od", None),
        P("od"),
        P(("od", "lk")),
        P(("od", "lk")),
        P("od", None),
        P("od", None),
        P("od", None),
        P("od", None, None, None),
    )
    out_specs = (P(("od", "lk"), None), P(("od", "lk")))
    return jax.shard_map(
        per_device, mesh=mesh, in_specs=in_specs, out_specs=out_specs, check_vma=False
    )
```

profile of v0, /device:TPU:0, one launch (start us, length us, event | category | flops | bytes accessed | tf_op | source)
XLA Modules:
  0.0 381.5 jit_solution(5252055032549368444)
XLA Ops:
  10.0 7.4 %all-to-all-start = ((s32[16,1,8]{2,1,0:T(1,128)}), s32[16,1,8]{2,1,0:T(1,128)S(1)}, u32[]{:S(2)}, u32[]{:S(2)}) async-start(s32[16,1,8]{2,1,0:T(1,128)} %bitcast.39), calls=%async_computation | async-start | bytes 16384 | tf_op jit(solution)/shard_map/all_to_all | solution.py:25
  17.4 6.3 %all-to-all-done = s32[16,1,8]{2,1,0:T(1,128)S(1)} async-done(((s32[16,1,8]{2,1,0:T(1,128)}), s32[16,1,8]{2,1,0:T(1,128)S(1)}, u32[]{:S(2)}, u32[]{:S(2)}) %all-to-all-start) | async-done | bytes 544 | tf_op jit(solution)/shard_map/all_to_all | solution.py:25
  24.0 8.6 %gather_fusion = bf16[128,128,256]{2,1,0:T(8,128)(2,1)} fusion(bf16[64,128,256]{2,1,0:T(8,128)(2,1)} %bitcast.89, s32[1024]{0:T(1024)S(1)} %pad_clamp_fusion.1), kind=kCustom, calls=%fused_computation | custom fusion | bytes 16777728 | tf_op jit(solution)/shard_map/gather | solution.py:44
  32.6 11.9 %copy.33 = bf16[128,128,256]{1,2,0:T(8,128)(2,1)} copy(bf16[128,128,256]{2,1,0:T(8,128)(2,1)} %gather_fusion) | data formatting | bytes 16777216 | tf_op jit(solution)/shard_map/gather | solution.py:44
  45.8 3.5 all-to-all-start.3
  49.3 4.8 %dynamic-slice_bitcast_fusion = bf16[16,8,128,128]{3,2,1,0:T(8,128)(2,1)} fusion(bf16[16,8,128,256]{2,3,1,0:T(8,128)(2,1)} %bitcast.90, s32[]{:T(128)S(6)} %select_n.42), kind=kLoop, calls=%fused_computation.7 | loop fusion | bytes 8388612 | tf_op jit(solution)/shard_map/transpose | solution.py:45
  54.1 1.8 all-to-all-done.3
  55.9 4.5 %all-to-all-start.1 = ((bf16[16,8,128,128]{3,2,1,0:T(8,128)(2,1)}), bf16[16,8,128,128]{3,2,1,0:T(8,128)(2,1)}, u32[]{:S(2)}, u32[]{:S(2)}) async-start(bf16[16,8,128,128]{3,2,1,0:T(8,128)(2,1)} %dynamic-slice_bitcast_fusion), calls=%async_computation.1 | async-start | bytes 8388608 | tf_op jit(solution)/shard_map/all_to_all | solution.py:48
  62.4 75.6 %all-to-all-done.1 = bf16[16,8,128,128]{3,2,1,0:T(8,128)(2,1)} async-done(((bf16[16,8,128,128]{3,2,1,0:T(8,128)(2,1)}), bf16[16,8,128,128]{3,2,1,0:T(8,128)(2,1)}, u32[]{:S(2)}, u32[]{:S(2)}) %all-to-all-start.1) | async-done | bytes 4194336 | tf_op jit(solution)/shard_map/all_to_all | solution.py:48
  138.0 4.3 %gather_fusion.1 = bf16[64,128,128]{2,1,0:T(8,128)(2,1)} fusion(bf16[128,128,128]{2,1,0:T(8,128)(2,1)} %bitcast.5, s32[1024]{0:T(1024)S(1)} %pad_clamp_fusion), kind=kCustom, calls=%fused_computation.1 | custom fusion | bytes 4194560 | tf_op jit(solution)/shard_map/gather | solution.py:51
  142.3 3.2 multiply_reduce_fusion
  146.5 3.5 all-to-all-start.2
  150.3 8.9 %all-to-all-done.2 = f32[128,2,512]{0,2,1:T(8,128)S(1)} async-done(((f32[128,2,512]{0,2,1:T(8,128)}), f32[128,2,512]{0,2,1:T(8,128)S(1)}, u32[]{:S(2)}, u32[]{:S(2)}) %all-to-all-start.2) | async-done | bytes 524320 | tf_op jit(solution)/shard_map/all_to_all | solution.py:62
  163.5 53.8 %psum.15 = f32[256]{0:T(256)S(1)} all-reduce(f32[256]{0:T(256)S(1)} %bitcast.103), channel_id=1, replica_groups=mesh['od'=16,'lk'=2] {'od','lk'}, use_global_device_ids=true, to_apply=%region_9.10 | all-reduce | flops 256 | bytes 2048 | tf_op jit(solution)/shard_map/psum | solution.py:79
  217.3 84.2 %all-reduce.3.cloned.1.call-done = f32[256,256]{0,1:T(8,128)} async-done(((f32[256,256]{0,1:T(8,128)}), f32[256,256]{0,1:T(8,128)}) %all-reduce.3.cloned.1.call-update) | async-done | bytes 262160 | tf_op jit(solution)/shard_map/psum | solution.py:79
  303.7 11.7 %cholesky.50 = f32[128,128]{1,0:T(8,128)S(1)} custom-call(f32[128,128]{1,0:T(8,128)S(1)} %cholesky.118), custom_call_target="Cholesky" | custom-call | tf_op jit(solution)/shard_map/jit(cholesky)/cholesky | solution.py:81
  315.4 9.8 %custom-call.15 = f32[1,128,128]{1,2,0:T(8,128)S(1)} custom-call(f32[1,128,128]{2,1,0:T(8,128)S(1)} %get-tuple-element.23), custom_call_target="InvertDiagBlocksLowerTriangular" | custom-call | tf_op jit(solution)/shard_map/jit(cholesky)/cholesky | solution.py:81
  325.7 11.7 %cholesky.105 = f32[128,128]{1,0:T(8,128)S(1)} custom-call(f32[128,128]{1,0:T(8,128)S(1)} %convolution_subtract_fusion.1), custom_call_target="Cholesky" | custom-call | tf_op jit(solution)/shard_map/jit(cholesky)/cholesky | solution.py:81
  339.5 5.2 %while.1 = (s32[]{:T(128)}, f32[256,256]{1,0:T(8,128)S(1)}, s32[2,2]{1,0:T(2,128)S(1)}, f32[2,128,128]{2,1,0:T(8,128)}, s32[]{:T(128)}) while((s32[]{:T(128)}, f32[256,256]{1,0:T(8,128)S(1)}, s32[2,2]{1,0:T(2,128)S(1)}, f32[2,128,128]{2,1,0:T(8,128)}, s32[]{:T(128)}) %tuple.27), condition=%wide.while_cond, body=%wide.while_body.sunk | while | flops 2 | bytes 132705 | solution.py:82
  340.1 2.0 bitcast_dynamic-update-slice_fusion.2
  342.8 2.0 bitcast_dynamic-update-slice_fusion.2
  344.8 20.5 %custom-call.16 = f32[2,128,128]{1,2,0:T(8,128)S(1)} custom-call(f32[2,128,128]{2,1,0:T(8,128)} %get-tuple-element.9), custom_call_target="InvertDiagBlocksLowerTriangular" | custom-call | tf_op jit(solution)/shard_map/jit(_solve_triangular)/triangular_solve | solution.py:82
  366.8 5.5 %fusion.2 = f32[4096,256]{1,0:T(8,128)} fusion(bf16[8192,256]{1,0:T(8,128)(2,1)} %param.8, s32[]{:T(128)S(6)} %select_n.39, f32[128,256]{1,0:T(8,128)S(1)} %fusion.10, f32[128,256]{1,0:T(8,128)S(1)} %fusion.6), kind=kOutput, calls=%fused_computation.10 | convolution fusion | flops 3221291008 | bytes 6553604 | tf_op jit(solution)/shard_map/dot_general | solution.py:93
  372.3 2.3 fusion
  (67 shorter events, 17.9 us)
Async XLA Ops:
  7.2 54.1 %copy-start = (bf16[8,8,128,128]{3,2,1,0:T(8,128)(2,1)S(1)}, bf16[8,8,128,128]{3,2,1,0:T(8,128)(2,1)}, u32[]{:S(2)}) copy-start(bf16[8,8,128,128]{3,2,1,0:T(8,128)(2,1)} %param.15) | copy-start | bytes 6291460
  10.0 13.7 %all-to-all-start = ((s32[16,1,8]{2,1,0:T(1,128)}), s32[16,1,8]{2,1,0:T(1,128)S(1)}, u32[]{:S(2)}, u32[]{:S(2)}) async-start(s32[16,1,8]{2,1,0:T(1,128)} %bitcast.39), calls=%async_computation | async-start | bytes 16384 | tf_op jit(solution)/shard_map/all_to_all | solution.py:25
  32.6 11.9 %copy-start.2 = (bf16[8192]{0:T(1024)(128)(2,1)S(1)}, bf16[8192]{0:T(1024)(128)(2,1)}, u32[]{:S(2)}) copy-start(bf16[8192]{0:T(1024)(128)(2,1)} %param.9) | copy-start | bytes 49156
  45.8 10.1 %all-to-all-start.3 = ((bf16[16,8,128]{2,1,0:T(8,128)(2,1)}), bf16[16,8,128]{2,1,0:T(8,128)(2,1)S(1)}, u32[]{:S(2)}, u32[]{:S(2)}) async-start(bf16[16,8,128]{2,1,0:T(8,128)(2,1)} %bitcast.21), calls=%async_computation.3 | async-start | bytes 65536 | tf_op jit(solution)/shard_map/all_to_all | solution.py:49
  54.1 6.3 %copy-start.4 = (s32[8,8]{1,0:T(8,128)S(1)}, s32[8,8]{1,0:T(8,128)}, u32[]{:S(2)}) copy-start(s32[8,8]{1,0:T(8,128)} %param.12) | copy-start | bytes 772
  54.1 6.4 %copy-start.5 = (s32[8,8]{1,0:T(8,128)S(1)}, s32[8,8]{1,0:T(8,128)}, u32[]{:S(2)}) copy-start(s32[8,8]{1,0:T(8,128)} %param.14) | copy-start | bytes 772
  55.9 82.1 %all-to-all-start.1 = ((bf16[16,8,128,128]{3,2,1,0:T(8,128)(2,1)}), bf16[16,8,128,128]{3,2,1,0:T(8,128)(2,1)}, u32[]{:S(2)}, u32[]{:S(2)}) async-start(bf16[16,8,128,128]{3,2,1,0:T(8,128)(2,1)} %dynamic-slice_bitcast_fusion), calls=%async_computation.1 | async-start | bytes 8388608 | tf_op jit(solution)/shard_map/all_to_all | solution.py:48
  142.3 7.8 %copy-start.3 = (f32[512]{0:T(512)S(1)}, f32[512]{0:T(512)}, u32[]{:S(2)}) copy-start(f32[512]{0:T(512)} %param.11) | copy-start | bytes 6148
  142.3 7.8 %copy-start.6 = (f32[512]{0:T(512)S(1)}, f32[512]{0:T(512)}, u32[]{:S(2)}) copy-start(f32[512]{0:T(512)} %param.10) | copy-start | bytes 6148
  146.5 12.7 %all-to-all-start.2 = ((f32[128,2,512]{0,2,1:T(8,128)}), f32[128,2,512]{0,2,1:T(8,128)S(1)}, u32[]{:S(2)}, u32[]{:S(2)}) async-start(f32[128,2,512]{0,2,1:T(8,128)} %bitcast.10), calls=%async_computation.2 | async-start | bytes 1048576 | tf_op jit(solution)/shard_map/all_to_all | solution.py:62
  150.0 151.5 %all-reduce.3.cloned.1.call-start = ((), (), s32[]{:S(2)}) async-start(), calls=%async_computation.4 | async-start | bytes 524288 | tf_op jit(solution)/shard_map/psum | solution.py:79
  365.2 7.0 %copy-start.1 = (bf16[8192,256]{1,0:T(8,128)(2,1)S(1)}, bf16[8192,256]{1,0:T(8,128)(2,1)}, u32[]{:S(2)}) copy-start(bf16[8192,256]{1,0:T(8,128)(2,1)} %param.8) | copy-start | bytes 12582916
Sparse Core Ops, SparseCore 0:
  162.8 138.6 all-reduce.2
where the time goes:
time: 383 us; the launch traced here: 381 us
  waiting for transfers between devices  177 us (46%)
  other arithmetic  58.8 us (15%)
  blocking collectives  53.8 us (14%)
  local copies, waits for them, and re-layouts  41.5 us (11%)
  starting transfers between devices  18.9 us (5%)
  matrix products  16 us (4%)
  between operations  15.6 us (4%)
    psum x1, waiting for transfers between devices, per_device(): gram, projected = lax.psum((gram_local, projected_local), ('od', 'lk'))  84.2 us
    all_to_all x1, waiting for transfers between devices, per_device(): lax.all_to_all(sent_factor, 'od', split_axis=0, concat_axis=0, tiled=True)  75.6 us
    psum x1, blocking collectives, per_device(): gram, projected = lax.psum((gram_local, projected_local), ('od', 'lk'))  53.8 us
    another operation x6, other arithmetic, per_device(): lower = jnp.linalg.cholesky(identity + gram)  34 us
    gather x2, local copies, waits for them, and re-layouts, per_device(): fac_rows[incoming]  20.5 us
    another operation x3, other arithmetic, per_device(): inverse = jax.scipy.linalg.solve_triangular(lower, identity, lower=True)  20.5 us
    all_to_all x1, waiting for transfers between devices, per_device(): lax.all_to_all(linked_part, 'lk', split_axis=1, concat_axis=0, tiled=True)  8.93 us
  transfers between devices with their start and end apart: 5, of which 5 were waited for; matrix products, arithmetic and copies ran while one was open for 2% of the time, Pallas kernels for 0%

commit v1 on v0

v1 whole, which is shorter than its diff:
```python
import functools

import jax
import jax.numpy as jnp
from jax import lax
from jax.experimental import pallas as pl
from jax.experimental.pallas import tpu as pltpu
from jax.sharding import PartitionSpec as P

MESH = pl.DeviceIdType.MESH
HIGHEST = lax.Precision.HIGHEST
VMEM = pltpu.VMEM


def dot(a, b, contract, precision=None):
    return lax.dot_general(
        a, b, (contract, ((), ())), precision=precision, preferred_element_type=jnp.float32
    )


def link_kernel(
    n, tiles, nb, owner_ref, local_ref, ecmp_ref, mean_ref, counts_ref, std_ref,
    fac_ref, route_hbm, out_ref,
    ask, got_ask, ask_smem, send_f, got_f, send_m, got_m, route, white,
    ask_send, ask_recv, f_send, f_recv, m_send, m_recv, local_sem, route_sem,
):
    me = lax.axis_index("od")
    first = lax.axis_index("lk") * tiles
    rank = fac_ref.shape[2]

    load_route = pltpu.make_async_copy(route_hbm.at[pl.ds(first, tiles)], route, route_sem)
    load_route.start()

    barrier = pltpu.get_barrier_semaphore()

    def greet(step, carry):
        peer = lax.rem(me + step, n)
        pl.semaphore_signal(barrier, inc=1, device_id={"od": peer}, device_id_type=MESH)
        return carry

    lax.fori_loop(1, n, greet, 0)

    owner_iota = lax.broadcasted_iota(jnp.int32, ask.shape, 0)
    lane = lax.broadcasted_iota(jnp.int32, ask.shape, 2)
    table = jnp.zeros(ask.shape, jnp.int32)
    for t in range(tiles):
        for k in range(nb):
            hit = (owner_iota == owner_ref[first + t, k]) & (lane == t)
            table = jnp.where(hit, local_ref[first + t, k], table)
    ask[...] = table
    send_m[...] = jnp.zeros_like(send_m)
    pl.semaphore_wait(barrier, n - 1)

    def push(src, dst, send_sem, recv_sem, at, peer):
        return pltpu.make_async_remote_copy(
            src_ref=src, dst_ref=dst.at[at], send_sem=send_sem.at[peer],
            recv_sem=recv_sem.at[at], device_id={"od": peer}, device_id_type=MESH,
        )

    def ask_peer(step, carry):
        peer = lax.rem(me + step, n)
        push(ask.at[peer], got_ask, ask_send, ask_recv, me, peer).start()
        return carry

    lax.fori_loop(1, n, ask_peer, 0)
    got_ask[me] = ask[me]

    def await_ask(step, carry):
        peer = lax.rem(me + step, n)
        push(ask.at[peer], got_ask, ask_send, ask_recv, peer, peer).wait_recv()
        return carry

    lax.fori_loop(1, n, await_ask, 0)
    to_smem = pltpu.make_async_copy(got_ask, ask_smem, local_sem)
    to_smem.start()
    to_smem.wait()

    def serve(step, carry):
        peer = lax.rem(me + step, n)
        for t in range(tiles):
            index = ask_smem[peer, 0, t]
            send_f[peer, t] = fac_ref[index]
            send_m[peer, t:t + 1] = mean_ref[index]
        push(send_m.at[peer], got_m, m_send, m_recv, me, peer).start()
        push(send_f.at[peer], got_f, f_send, f_recv, me, peer).start()
        return carry

    lax.fori_loop(1, n, serve, 0)
    own_m = jnp.zeros((1,) + send_m.shape[1:], jnp.float32)
    got_m[me] = own_m[0]
    for t in range(tiles):
        index = ask_smem[me, 0, t]
        got_f[me, t] = fac_ref[index]
        got_m[me, t:t + 1] = mean_ref[index]
    spread = [jnp.broadcast_to(std_ref[t:t + 1, :], (128, 128)).T for t in range(tiles)]
    load_route.wait()

    def await_blocks(step, carry):
        peer = lax.rem(me + step, n)
        push(send_m.at[peer], got_m, m_send, m_recv, peer, peer).wait_recv()
        push(send_f.at[peer], got_f, f_send, f_recv, peer, peer).wait_recv()
        return carry

    lax.fori_loop(1, n, await_blocks, 0)

    gram = jnp.zeros((rank, rank), jnp.float32)
    projected = jnp.zeros((8, rank), jnp.float32)
    for t in range(tiles):
        linked = jnp.zeros((128, rank), jnp.float32)
        predicted = jnp.zeros((8, 128), jnp.float32)
        for k in range(nb):
            owner = owner_ref[first + t, k]
            times = ecmp_ref[first + t, k].astype(jnp.float32)
            share = route[t, k]
            linked += times * dot(share, got_f[owner, t], ((1,), (0,)))
            predicted += times * dot(got_m[owner].astype(jnp.bfloat16), share, ((1,), (1,)))
        noise = jnp.concatenate([spread[t]] * (rank // 128), axis=1)
        whitened = linked / noise
        innovation = (counts_ref[t:t + 1, :] - predicted[t:t + 1, :]) / std_ref[t:t + 1, :]
        white[t * 128:(t + 1) * 128, :] = whitened
        projected += dot(
            jnp.broadcast_to(innovation, (8, 128)), whitened, ((1,), (0,)), HIGHEST
        )
    whole = white[...]
    gram = dot(whole.T, whole, ((1,), (0,)), HIGHEST)
    row = lax.broadcasted_iota(jnp.int32, (8, rank), 0)
    column = lax.broadcasted_iota(jnp.int32, (8, rank), 1)
    head = gram[0:8, :]
    head = jnp.where((row == 0) & (column > 0), projected, head)
    head = jnp.where((row == 1) & (column == rank - 1), projected[:, 0:1], head)
    out_ref[...] = gram
    out_ref[0:8, :] = head

    def drain(step, carry):
        peer = lax.rem(me + step, n)
        push(ask.at[peer], got_ask, ask_send, ask_recv, me, peer).wait_send()
        push(send_m.at[peer], got_m, m_send, m_recv, me, peer).wait_send()
        push(send_f.at[peer], got_f, f_send, f_recv, me, peer).wait_send()
        return carry

    lax.fori_loop(1, n, drain, 0)


def sum_kernel(n_od, n_lk, in_ref, out_ref, got, full, send1, recv1, send2, recv2):
    n = n_od * n_lk
    me = lax.axis_index("od") * n_lk + lax.axis_index("lk")

    def place(step):
        peer = lax.rem(me + step, n)
        return peer, {"od": peer // n_lk, "lk": lax.rem(peer, n_lk)}

    barrier = pltpu.get_barrier_semaphore()

    def greet(step, carry):
        _, where = place(step)
        pl.semaphore_signal(barrier, inc=1, device_id=where, device_id_type=MESH)
        return carry

    lax.fori_loop(1, n, greet, 0)
    pl.semaphore_wait(barrier, n - 1)

    def scatter(step, at_me):
        peer, where = place(step)
        at = me if at_me else peer
        return pltpu.make_async_remote_copy(
            src_ref=in_ref.at[peer], dst_ref=got.at[at], send_sem=send1.at[peer],
            recv_sem=recv1.at[at], device_id=where, device_id_type=MESH,
        )

    def gather(step, at_me):
        peer, where = place(step)
        at = me if at_me else peer
        return pltpu.make_async_remote_copy(
            src_ref=full.at[me], dst_ref=full.at[at], send_sem=send2.at[peer],
            recv_sem=recv2.at[at], device_id=where, device_id_type=MESH,
        )

    def every(action):
        def body(step, carry):
            action(step)
            return carry

        lax.fori_loop(1, n, body, 0)

    every(lambda step: scatter(step, True).start())
    got[me] = in_ref[me]
    every(lambda step: scatter(step, False).wait_recv())
    full[me] = jnp.sum(got[...], axis=0)
    every(lambda step: gather(step, True).start())
    every(lambda step: gather(step, False).wait_recv())
    out_ref[...] = full[...]
    every(lambda step: scatter(step, True).wait_send())
    every(lambda step: gather(step, True).wait_send())


@jax.jit
def inverse_factor(a):
    size = a.shape[0]
    lane = lax.broadcasted_iota(jnp.int32, (1, size), 1)
    sub = lax.broadcasted_iota(jnp.int32, (8, size), 0)
    lanes = lax.broadcasted_iota(jnp.int32, (8, size), 1)
    groups = [a[8 * g:8 * g + 8, :] for g in range(size // 8)]
    for j in range(size):
        at, offset = j // 8, j % 8
        here = lane == j
        row = groups[at][offset:offset + 1, :]
        scaled = jnp.where(here, 1.0, row) / row[:, j:j + 1]
        for g in range(at, size // 8):
            if g == at and offset == 7:
                continue
            old = groups[g]
            new = jnp.where(here, 0.0, old) - old[:, j:j + 1] * scaled
            groups[g] = jnp.where(sub > offset, new, old) if g == at else new
    done = []
    for g, rows in enumerate(groups):
        diagonal = lanes == sub + 8 * g
        pivot = jnp.sum(jnp.where(diagonal, rows, 0.0), axis=1, keepdims=True)
        unit = jnp.where(diagonal, 1.0, jnp.where(lanes < sub + 8 * g, rows, 0.0))
        done.append(unit * lax.rsqrt(pivot))
    return jnp.concatenate(done, axis=0)


def update_kernel(start_ref, gram_ref, fac_ref, new_ref, corr_ref, high, low, gain):
    rank = gram_ref.shape[0]
    half = rank // 2

    @pl.when(pl.program_id(0) == 0)
    def _():
        lane = lax.broadcasted_iota(jnp.int32, (half, half), 1)
        sub = lax.broadcasted_iota(jnp.int32, (half, half), 0)

        def symmetric(block):
            upper = block.T
            return jnp.where(sub >= lane, block, upper) + jnp.where(sub == lane, 1.0, 0.0)

        a11 = symmetric(gram_ref[:half, :half])
        a21 = gram_ref[half:, :half]
        w1 = inverse_factor(a11)
        l21 = dot(a21, w1, ((1,), (1,)), HIGHEST)
        a22 = symmetric(gram_ref[half:, half:]) - dot(l21, l21, ((1,), (1,)), HIGHEST)
        w2 = inverse_factor(a22)
        w21 = -dot(w2, dot(l21, w1, ((1,), (0,)), HIGHEST), ((1,), (0,)), HIGHEST)
        inverse = jnp.concatenate(
            [jnp.concatenate([w1, jnp.zeros((half, half), jnp.float32)], axis=1),
             jnp.concatenate([w21, w2], axis=1)], axis=0,
        )
        lane = lax.broadcasted_iota(jnp.int32, (8, rank), 1)
        projected = jnp.broadcast_to(gram_ref[0:1, :], (8, rank))
        projected = jnp.where(lane == 0, gram_ref[1:2, rank - 1:rank], projected)
        inner = dot(projected, inverse, ((1,), (1,)), HIGHEST)
        vector = dot(inner, inverse, ((1,), (0,)), HIGHEST)
        top = vector.astype(jnp.bfloat16)
        rest = vector - top.astype(jnp.float32)
        middle = rest.astype(jnp.bfloat16)
        last = (rest - middle.astype(jnp.float32)).astype(jnp.bfloat16)
        gain[...] = jnp.concatenate([top, middle, last], axis=0)
        turned = inverse.T
        upper = turned.astype(jnp.bfloat16)
        high[...] = upper
        low[...] = (turned - upper.astype(jnp.float32)).astype(jnp.bfloat16)

    rows = fac_ref[...]
    new_ref[...] = dot(rows, high[...], ((1,), (0,))) + dot(rows, low[...], ((1,), (0,)))
    parts = dot(gain[...], rows, ((1,), (1,)))
    corr_ref[0] = parts[0:1] + parts[8:9] + parts[16:17]


def per_device(factor, prior_mean, counts, noise_std, owner_ids, local_ids, ecmp, route_share):
    n_od, n_lk = lax.axis_size("od"), lax.axis_size("lk")
    group_tiles, nb = owner_ids.shape
    tiles = group_tiles // n_lk
    link_rows, block_rows = route_share.shape[2:]
    rank = factor.shape[1]
    blocks = factor.shape[0] // block_rows
    vmem = pl.BlockSpec(memory_space=VMEM)
    smem = pl.BlockSpec(memory_space=pltpu.SMEM)
    dma = pltpu.SemaphoreType.DMA

    packed = pl.pallas_call(
        functools.partial(link_kernel, n_od, tiles, nb),
        out_shape=jax.ShapeDtypeStruct((rank, rank), jnp.float32),
        in_specs=[smem, smem, smem, vmem, vmem, vmem, vmem, pl.BlockSpec(memory_space=pl.ANY)],
        out_specs=vmem,
        scratch_shapes=[
            VMEM((n_od, 8, 128), jnp.int32),
            VMEM((n_od, 8, 128), jnp.int32),
            pltpu.SMEM((n_od, 8, 128), jnp.int32),
            VMEM((n_od, tiles, block_rows, rank), jnp.bfloat16),
            VMEM((n_od, tiles, block_rows, rank), jnp.bfloat16),
            VMEM((n_od, 8, block_rows), jnp.float32),
            VMEM((n_od, 8, block_rows), jnp.float32),
            VMEM((tiles, nb, link_rows, block_rows), jnp.bfloat16),
            VMEM((tiles * link_rows, rank), jnp.float32),
        ] + [dma((n_od,))] * 6 + [dma, dma],
        compiler_params=pltpu.CompilerParams(
            collective_id=0, has_side_effects=True, vmem_limit_bytes=56 * 1024 * 1024
        ),
        name="links",
    )(
        owner_ids, local_ids, ecmp,
        prior_mean.astype(jnp.float32).reshape(blocks, 1, block_rows),
        counts.reshape(tiles, link_rows), noise_std.reshape(tiles, link_rows),
        factor.reshape(blocks, block_rows, rank), route_share,
    )

    n_all = n_od * n_lk
    slab = (n_all, rank // n_all, rank)
    summed = pl.pallas_call(
        functools.partial(sum_kernel, n_od, n_lk),
        out_shape=jax.ShapeDtypeStruct(slab, jnp.float32),
        in_specs=[vmem],
        out_specs=vmem,
        scratch_shapes=[VMEM(slab, jnp.float32), VMEM(slab, jnp.float32)]
        + [dma((n_all,))] * 4,
        compiler_params=pltpu.CompilerParams(
            collective_id=1, has_side_effects=True, vmem_limit_bytes=32 * 1024 * 1024
        ),
        name="sums",
    )(packed.reshape(slab)).reshape(rank, rank)

    own_rows = factor.shape[0] // n_lk
    step_rows = min(512, own_rows)
    steps = own_rows // step_rows
    start = (lax.axis_index("lk") * steps).astype(jnp.int32).reshape(1)
    new_factor, correction = pl.pallas_call(
        update_kernel,
        out_shape=(
            jax.ShapeDtypeStruct((own_rows, rank), jnp.float32),
            jax.ShapeDtypeStruct((steps, 1, step_rows), jnp.float32),
        ),
        grid_spec=pltpu.PrefetchScalarGridSpec(
            num_scalar_prefetch=1,
            grid=(steps,),
            in_specs=[
                pl.BlockSpec((rank, rank), lambda i, start: (0, 0)),
                pl.BlockSpec((step_rows, rank), lambda i, start: (start[0] + i, 0)),
            ],
            out_specs=[
                pl.BlockSpec((step_rows, rank), lambda i, start: (i, 0)),
                pl.BlockSpec((1, 1, step_rows), lambda i, start: (i, 0, 0)),
            ],
            scratch_shapes=[
                VMEM((rank, rank), jnp.bfloat16),
                VMEM((rank, rank), jnp.bfloat16),
                VMEM((24, rank), jnp.bfloat16),
            ],
        ),
        compiler_params=pltpu.CompilerParams(vmem_limit_bytes=32 * 1024 * 1024),
        name="update",
    )(start, summed, factor)
    return (new_factor, correction.reshape(-1))


def solution(mesh):
    in_specs = (
        P("od", None),
        P("od"),
        P(("od", "lk")),
        P(("od", "lk")),
        P("od", None),
        P("od", None),
        P("od", None),
        P("od", None, None, None),
    )
    out_specs = (P(("od", "lk"), None), P(("od", "lk")))
    return jax.shard_map(
        per_device, mesh=mesh, in_specs=in_specs, out_specs=out_specs, check_vma=False
    )
```

time: 383 us -> 160 us (0.42)
  waiting for transfers between devices: 177 us -> 0 us
  Pallas kernels: 0 us -> 157 us
  other arithmetic: 58.8 us -> 1.49 us
  blocking collectives: 53.8 us -> 0 us
  local copies, waits for them, and re-layouts: 41.5 us -> 0.95 us
  starting transfers between devices: 18.9 us -> 0 us
  matrix products: 16 us -> 0 us
  between operations: 15.6 us -> 0.67 us
    pallas_call x0 -> x3, Pallas kernels: none -> 157 us  [the longest x1 83.2 us: per_device(): pl.pallas_call(functools.partial(link_kernel, n_od, tiles, nb), out_shape...]
    all_to_all x4 -> x0, waiting for transfers between devices: 92.6 us -> none  [the longest x1 75.6 us: per_device(): lax.all_to_all(sent_factor, 'od', split_axis=0, concat_axis=0, tiled=True)]
    psum x1 -> x0, waiting for transfers between devices: 84.2 us -> none  [per_device(): gram, projected = lax.psum((gram_local, projected_local), ('od', 'lk'))]
    another operation x9 -> x0, other arithmetic: 54.5 us -> none  [the longest x6 34 us: per_device(): lower = jnp.linalg.cholesky(identity + gram)]
    psum x1 -> x0, blocking collectives: 53.8 us -> none  [per_device(): gram, projected = lax.psum((gram_local, projected_local), ('od', 'lk'))]
    gather x5 -> x0, local copies, waits for them, and re-layouts: 26.8 us -> none  [the longest x2 20.5 us: per_device(): fac_rows[incoming]]
    all_to_all x4 -> x0, starting transfers between devices: 18.9 us -> none  [the longest x1 7.36 us: requests_for(): lax.all_to_all(asking, 'od', split_axis=0, concat_axis=0, tiled=True)]
    dot_general x8 -> x0, matrix products: 14.6 us -> none  [the longest x1 5.49 us: per_device(): jnp.dot(own_rows, inverse.T, precision=lax.Precision.HIGHEST, preferred_e...]
  transfers between devices with their start and end apart: 5 -> 0, of which waited for: 5 -> 0; matrix products, arithmetic and copies ran while one was open for 2% -> 0% of each run, Pallas kernels for 0% -> 0%
where the time goes in v1:
time: 160 us
  Pallas kernels  157 us (98%)
    pallas_call x1, Pallas kernels, per_device(): pl.pallas_call(functools.partial(link_kernel, n_od, tiles, nb), out_shape...  83.2 us
    pallas_call x1, Pallas kernels, per_device(): pl.pallas_call(functools.partial(sum_kernel, n_od, n_lk), out_shape=jax.S...  45.2 us
    pallas_call x1, Pallas kernels, per_device(): pl.pallas_call(update_kernel, out_shape=(jax.ShapeDtypeStruct((own_rows,...  28.2 us

profile of v1, /device:TPU:0, one launch (start us, length us, event | category | flops | bytes accessed | tf_op | source)
XLA Modules:
  0.0 159.7 jit_solution(151352983206292799)
XLA Ops:
  0.6 0.0 copy-start
  0.6 1.5 reshape.39
  2.1 83.2 %links.1 = f32[256,256]{1,0:T(8,128)} custom-call(s32[8,8]{1,0:T(8,128)} %owner_ref.1, s32[8,8]{1,0:T(8,128)} %local_ref.1, s32[8,8]{1,0:T(8,128)} %ecmp_ref.1, f32[64,1,128]{2,1,0:T(1,128)} %bitcast.11, f32[4,128]{1,0:T(4,128)} %bitcast.12, f32[4,128]{1,0:T(4,128)} %bitcast.13, bf16[64,128,256]{2,1,0:T(8,128)(2,1)} %bitcast.8, ...), custom_call_target="tpu_custom_call" | custom-call | tf_op jit(solution)/shard_map/links/pallas_call | solution.py:279
  85.4 0.0 copy-start.1
  85.4 0.9 copy-done.1
  86.3 45.2 %sums.1 = f32[32,8,256]{2,1,0:T(8,128)S(1)} custom-call(f32[32,8,256]{2,1,0:T(8,128)S(1)} %bitcast.10), custom_call_target="tpu_custom_call" | custom-call | tf_op jit(solution)/shard_map/sums/pallas_call | solution.py:308
  131.5 0.0 copy-done
  131.5 28.2 %update.1 = (f32[4096,256]{1,0:T(8,128)}, f32[8,1,512]{2,1,0:T(1,128)}) custom-call(s32[1]{0:T(128)} %bitcast.start_ref, f32[256,256]{1,0:T(8,128)S(1)} %bitcast.9, bf16[8192,256]{1,0:T(8,128)(2,1)S(1)} %copy-done), custom_call_target="tpu_custom_call" | custom-call | tf_op jit(solution)/shard_map/update/pallas_call | solution.py:325
Async XLA Ops:
  0.6 130.9 %copy-start = (bf16[8192,256]{1,0:T(8,128)(2,1)S(1)}, bf16[8192,256]{1,0:T(8,128)(2,1)}, u32[]{:S(2)}) copy-start(bf16[8192,256]{1,0:T(8,128)(2,1)} %fac_ref.1) | copy-start | bytes 12582916
  85.4 1.0 copy-start.1

commit v2 on v1

v2 whole, which is shorter than its diff:
```python
import functools

import jax
import jax.numpy as jnp
from jax import lax
from jax.experimental import pallas as pl
from jax.experimental.pallas import tpu as pltpu
from jax.sharding import PartitionSpec as P

MESH = pl.DeviceIdType.MESH
HIGHEST = lax.Precision.HIGHEST
VMEM = pltpu.VMEM


def dot(a, b, contract, precision=None):
    return lax.dot_general(
        a, b, (contract, ((), ())), precision=precision, preferred_element_type=jnp.float32
    )


def split(a):
    high = a.astype(jnp.bfloat16)
    return high, (a - high.astype(jnp.float32)).astype(jnp.bfloat16)


def link_kernel(
    n, n_lk, tiles, nb, owner_ref, local_ref, ecmp_ref, mean_ref, counts_ref, std_ref,
    fac_ref, route_hbm, out_ref,
    ask, got_ask, ask_smem, send_f, got_f, send_m, got_m, route, linked, predicted,
    sums, got_s, full,
    ask_send, ask_recv, f_send, f_recv, m_send, m_recv, s_send, s_recv, t_send, t_recv,
    local_sem, route_sem,
):
    me, my_lk = lax.axis_index("od"), lax.axis_index("lk")
    first = my_lk * tiles
    rank = fac_ref.shape[2]
    n_all = n * n_lk
    me_all = me * n_lk + my_lk
    half = n // 2

    load_route = pltpu.make_async_copy(route_hbm.at[pl.ds(first, tiles)], route, route_sem)
    load_route.start()

    barrier = pltpu.get_barrier_semaphore()

    def loop(start, stop, action):
        def body(step, carry):
            action(step)
            return carry

        lax.fori_loop(start, stop, body, 0)

    def place(index):
        return {"od": index // n_lk, "lk": lax.rem(index, n_lk)}

    def greet(step):
        where = place(lax.rem(me_all + step, n_all))
        pl.semaphore_signal(barrier, inc=1, device_id=where, device_id_type=MESH)

    loop(1, n_all, greet)

    owner_iota = lax.broadcasted_iota(jnp.int32, ask.shape, 0)
    lane = lax.broadcasted_iota(jnp.int32, ask.shape, 2)
    table = jnp.zeros(ask.shape, jnp.int32)
    for t in range(tiles):
        for k in range(nb):
            hit = (owner_iota == owner_ref[first + t, k]) & (lane == t)
            table = jnp.where(hit, local_ref[first + t, k], table)
    ask[...] = table
    send_m[...] = jnp.zeros_like(send_m)
    linked[...] = jnp.zeros_like(linked)
    predicted[...] = jnp.zeros_like(predicted)
    pl.semaphore_wait(barrier, n_all - 1)

    def push(src, dst, send_sem, recv_sem, at, peer):
        return pltpu.make_async_remote_copy(
            src_ref=src, dst_ref=dst.at[at], send_sem=send_sem.at[peer],
            recv_sem=recv_sem.at[at], device_id={"od": peer}, device_id_type=MESH,
        )

    def far(step):
        return (1 - me // half) * half + lax.rem(me + step, half)

    def near(step):
        return (me // half) * half + lax.rem(me + step, half)

    def others(action, far_first):
        if far_first:
            loop(0, half, lambda step: action(far(step)))
        loop(1, half, lambda step: action(near(step)))
        if not far_first:
            loop(0, half, lambda step: action(far(step)))

    others(lambda peer: push(ask.at[peer], got_ask, ask_send, ask_recv, me, peer).start(), True)
    got_ask[me] = ask[me]
    others(
        lambda peer: push(ask.at[peer], got_ask, ask_send, ask_recv, peer, peer).wait_recv(), False
    )
    to_smem = pltpu.make_async_copy(got_ask, ask_smem, local_sem)
    to_smem.start()
    to_smem.wait()

    def serve(peer):
        for t in range(tiles):
            index = ask_smem[peer, 0, t]
            send_f[peer, t] = fac_ref[index]
            send_m[peer, t:t + 1] = mean_ref[index]
        push(send_m.at[peer], got_m, m_send, m_recv, me, peer).start()
        push(send_f.at[peer], got_f, f_send, f_recv, me, peer).start()

    others(serve, True)
    got_m[me] = jnp.zeros(send_m.shape[1:], jnp.float32)
    for t in range(tiles):
        index = ask_smem[me, 0, t]
        got_f[me, t] = fac_ref[index]
        got_m[me, t:t + 1] = mean_ref[index]
    spread = [jnp.broadcast_to(std_ref[t:t + 1, :], (128, 128)).T for t in range(tiles)]
    load_route.wait()

    def use(owner):
        means = got_m[owner].astype(jnp.bfloat16)
        for t in range(tiles):
            slot, times = 0, 0
            for k in range(nb):
                named = owner_ref[first + t, k] == owner
                slot = jnp.where(named, k, slot)
                times = jnp.where(named, ecmp_ref[first + t, k], times)
            times = times.astype(jnp.float32)
            share = route[t, slot]
            linked[t] += times * dot(share, got_f[owner, t], ((1,), (0,)))
            predicted[t] += times * dot(means, share, ((1,), (1,)))

    def arrive(peer):
        push(send_m.at[peer], got_m, m_send, m_recv, peer, peer).wait_recv()
        push(send_f.at[peer], got_f, f_send, f_recv, peer, peer).wait_recv()
        use(peer)

    use(me)
    others(arrive, False)

    whole, innovation = [], []
    for t in range(tiles):
        whole.append(linked[t] / jnp.concatenate([spread[t]] * (rank // 128), axis=1))
        innovation.append(
            (counts_ref[t:t + 1, :] - predicted[t, t:t + 1, :]) / std_ref[t:t + 1, :]
        )
    high, low = split(jnp.concatenate(whole, axis=0))
    in_high, in_low = split(jnp.broadcast_to(
        jnp.concatenate(innovation, axis=1), (8, tiles * 128)
    ))
    cross = dot(high, low, ((0,), (0,)))
    gram = dot(high, high, ((0,), (0,))) + (cross + cross.T)
    projected = dot(in_high, high, ((1,), (0,))) + (
        dot(in_low, high, ((1,), (0,))) + dot(in_high, low, ((1,), (0,)))
    )
    mid = rank // 2
    row = lax.broadcasted_iota(jnp.int32, (mid, mid), 0)
    column = lax.broadcasted_iota(jnp.int32, (mid, mid), 1)
    last = gram[mid:, mid:]
    slabs = mid // 8
    sums[0:slabs, :, :mid] = gram[mid:, :mid].reshape(slabs, 8, mid)
    sums[0:slabs, :, mid:] = jnp.where(row >= column, gram[:mid, :mid], last).reshape(
        slabs, 8, mid
    )
    diagonal = jnp.sum(jnp.where(row == column, last, 0.0), axis=0, keepdims=True)
    diagonal = jnp.concatenate([diagonal, diagonal], axis=1)
    eight = lax.broadcasted_iota(jnp.int32, (8, rank), 0)
    sums[slabs] = jnp.where(eight == 0, projected, diagonal)

    stride = n_all // slabs
    summer = (me % stride == 0) | ((me == 1) & (my_lk == 0))
    mine = jnp.where(me % stride == 0, (me // stride) * n_lk + my_lk, slabs)

    def home(i):
        last_one = i // slabs
        return (
            (1 - last_one) * (i // n_lk) * stride + last_one,
            (1 - last_one) * lax.rem(i, n_lk),
        )

    def to_home(i):
        od, lk = home(i)
        return pltpu.make_async_remote_copy(
            src_ref=sums.at[i], dst_ref=got_s.at[me_all], send_sem=s_send.at[i],
            recv_sem=s_recv.at[me_all], device_id={"od": od, "lk": lk}, device_id_type=MESH,
        )

    def not_mine(action):
        def body(i):
            od, lk = home(i)

            @pl.when((od != me) | (lk != my_lk))
            def _():
                action(i)

        loop(0, slabs + 1, body)

    def from_home(step, i):
        peer = lax.rem(me_all + step, n_all)
        return pltpu.make_async_remote_copy(
            src_ref=full.at[i], dst_ref=full.at[i], send_sem=t_send.at[step],
            recv_sem=t_recv.at[i], device_id=place(peer), device_id_type=MESH,
        )

    def await_part(step):
        peer = lax.rem(me_all + step, n_all)
        pltpu.make_async_remote_copy(
            src_ref=sums.at[0], dst_ref=got_s.at[peer], send_sem=s_send.at[0],
            recv_sem=s_recv.at[peer], device_id=place(peer), device_id_type=MESH,
        ).wait_recv()

    not_mine(lambda i: to_home(i).start())

    @pl.when(summer)
    def _():
        got_s[me_all] = sums[mine]
        loop(1, n_all, await_part)
        full[mine] = jnp.sum(got_s[...], axis=0)
        loop(1, n_all, lambda step: from_home(step, mine).start())

    not_mine(lambda i: from_home(1, i).wait_recv())
    out_ref[...] = full[...]

    def drain(peer):
        push(ask.at[peer], got_ask, ask_send, ask_recv, me, peer).wait_send()
        push(send_m.at[peer], got_m, m_send, m_recv, me, peer).wait_send()
        push(send_f.at[peer], got_f, f_send, f_recv, me, peer).wait_send()

    others(drain, True)
    not_mine(lambda i: to_home(i).wait_send())

    @pl.when(summer)
    def _():
        loop(1, n_all, lambda step: from_home(step, mine).wait_send())


@jax.jit
def inverse_factor(a):
    size = a.shape[0]
    lane = lax.broadcasted_iota(jnp.int32, (1, size), 1)
    sub = lax.broadcasted_iota(jnp.int32, (8, size), 0)
    lanes = lax.broadcasted_iota(jnp.int32, (8, size), 1)
    groups = [a[8 * g:8 * g + 8, :] for g in range(size // 8)]
    for j in range(size):
        at, offset = j // 8, j % 8
        here = lane == j
        row = groups[at][offset:offset + 1, :]
        scaled = jnp.where(here, 1.0, row) / row[:, j:j + 1]
        for g in range(at, size // 8):
            if g == at and offset == 7:
                continue
            old = groups[g]
            new = jnp.where(here, 0.0, old) - old[:, j:j + 1] * scaled
            groups[g] = jnp.where(sub > offset, new, old) if g == at else new
    done = []
    for g, rows in enumerate(groups):
        diagonal = lanes == sub + 8 * g
        pivot = jnp.sum(jnp.where(diagonal, rows, 0.0), axis=1, keepdims=True)
        unit = jnp.where(diagonal, 1.0, jnp.where(lanes < sub + 8 * g, rows, 0.0))
        done.append(unit * lax.rsqrt(pivot))
    return jnp.concatenate(done, axis=0)


def update_kernel(start_ref, gram_ref, fac_ref, new_ref, corr_ref, high, low, gain):
    rank = gram_ref.shape[2]
    half = rank // 2
    slabs = half // 8

    @pl.when(pl.program_id(0) == 0)
    def _():
        lane = lax.broadcasted_iota(jnp.int32, (half, half), 1)
        sub = lax.broadcasted_iota(jnp.int32, (half, half), 0)

        packed = gram_ref[0:slabs].reshape(half, rank)
        a21, both = packed[:, :half], packed[:, half:]
        turned = both.T
        extra = gram_ref[slabs]
        a11 = jnp.where(sub >= lane, both, turned) + jnp.where(sub == lane, 1.0, 0.0)
        a22 = jnp.where(sub < lane, both, turned)
        a22 = jnp.where(sub == lane, 1.0 + extra[1:2, :half], a22)
        w1 = inverse_factor(a11)
        l21 = dot(a21, w1, ((1,), (1,)), HIGHEST)
        a22 = a22 - dot(l21, l21, ((1,), (1,)), HIGHEST)
        w2 = inverse_factor(a22)
        w21 = -dot(w2, dot(l21, w1, ((1,), (0,)), HIGHEST), ((1,), (0,)), HIGHEST)
        inverse = jnp.concatenate(
            [jnp.concatenate([w1, jnp.zeros((half, half), jnp.float32)], axis=1),
             jnp.concatenate([w21, w2], axis=1)], axis=0,
        )
        projected = jnp.broadcast_to(extra[0:1, :], (8, rank))
        inner = dot(projected, inverse, ((1,), (1,)), HIGHEST)
        vector = dot(inner, inverse, ((1,), (0,)), HIGHEST)
        top = vector.astype(jnp.bfloat16)
        rest = vector - top.astype(jnp.float32)
        middle = rest.astype(jnp.bfloat16)
        last = (rest - middle.astype(jnp.float32)).astype(jnp.bfloat16)
        gain[...] = jnp.concatenate([top, middle, last], axis=0)
        turned = inverse.T
        upper = turned.astype(jnp.bfloat16)
        high[...] = upper
        low[...] = (turned - upper.astype(jnp.float32)).astype(jnp.bfloat16)

    rows = fac_ref[...]
    new_ref[...] = dot(rows, high[...], ((1,), (0,))) + dot(rows, low[...], ((1,), (0,)))
    parts = dot(gain[...], rows, ((1,), (1,)))
    corr_ref[0] = parts[0:1] + parts[8:9] + parts[16:17]


def per_device(factor, prior_mean, counts, noise_std, owner_ids, local_ids, ecmp, route_share):
    n_od, n_lk = lax.axis_size("od"), lax.axis_size("lk")
    group_tiles, nb = owner_ids.shape
    tiles = group_tiles // n_lk
    link_rows, block_rows = route_share.shape[2:]
    rank = factor.shape[1]
    blocks = factor.shape[0] // block_rows
    vmem = pl.BlockSpec(memory_space=VMEM)
    smem = pl.BlockSpec(memory_space=pltpu.SMEM)
    dma = pltpu.SemaphoreType.DMA

    n_all = n_od * n_lk
    slabs = rank // 16 + 1
    slab = (slabs, 8, rank)
    summed = pl.pallas_call(
        functools.partial(link_kernel, n_od, n_lk, tiles, nb),
        out_shape=jax.ShapeDtypeStruct(slab, jnp.float32),
        in_specs=[smem, smem, smem, vmem, vmem, vmem, vmem, pl.BlockSpec(memory_space=pl.ANY)],
        out_specs=vmem,
        scratch_shapes=[
            VMEM((n_od, 8, 128), jnp.int32),
            VMEM((n_od, 8, 128), jnp.int32),
            pltpu.SMEM((n_od, 8, 128), jnp.int32),
            VMEM((n_od, tiles, block_rows, rank), jnp.bfloat16),
            VMEM((n_od, tiles, block_rows, rank), jnp.bfloat16),
            VMEM((n_od, 8, block_rows), jnp.float32),
            VMEM((n_od, 8, block_rows), jnp.float32),
            VMEM((tiles, nb, link_rows, block_rows), jnp.bfloat16),
            VMEM((tiles, link_rows, rank), jnp.float32),
            VMEM((tiles, 8, link_rows), jnp.float32),
            VMEM(slab, jnp.float32),
            VMEM((n_all, 8, rank), jnp.float32),
            VMEM(slab, jnp.float32),
        ] + [dma((n_od,))] * 6 + [dma((slabs,)), dma((n_all,)), dma((n_all,)), dma((slabs,))]
        + [dma, dma],
        compiler_params=pltpu.CompilerParams(
            collective_id=0, has_side_effects=True, vmem_limit_bytes=56 * 1024 * 1024
        ),
        name="links",
    )(
        owner_ids, local_ids, ecmp,
        prior_mean.astype(jnp.float32).reshape(blocks, 1, block_rows),
        counts.reshape(tiles, link_rows), noise_std.reshape(tiles, link_rows),
        factor.reshape(blocks, block_rows, rank), route_share,
    )

    own_rows = factor.shape[0] // n_lk
    step_rows = min(512, own_rows)
    steps = own_rows // step_rows
    start = (lax.axis_index("lk") * steps).astype(jnp.int32).reshape(1)
    new_factor, correction = pl.pallas_call(
        update_kernel,
        out_shape=(
            jax.ShapeDtypeStruct((own_rows, rank), jnp.float32),
            jax.ShapeDtypeStruct((steps, 1, step_rows), jnp.float32),
        ),
        grid_spec=pltpu.PrefetchScalarGridSpec(
            num_scalar_prefetch=1,
            grid=(steps,),
            in_specs=[
                pl.BlockSpec(slab, lambda i, start: (0, 0, 0)),
                pl.BlockSpec((step_rows, rank), lambda i, start: (start[0] + i, 0)),
            ],
            out_specs=[
                pl.BlockSpec((step_rows, rank), lambda i, start: (i, 0)),
                pl.BlockSpec((1, 1, step_rows), lambda i, start: (i, 0, 0)),
            ],
            scratch_shapes=[
                VMEM((rank, rank), jnp.bfloat16),
                VMEM((rank, rank), jnp.bfloat16),
                VMEM((24, rank), jnp.bfloat16),
            ],
        ),
        compiler_params=pltpu.CompilerParams(vmem_limit_bytes=32 * 1024 * 1024),
        name="update",
    )(start, summed, factor)
    return (new_factor, correction.reshape(-1))


def solution(mesh):
    in_specs = (
        P("od", None),
        P("od"),
        P(("od", "lk")),
        P(("od", "lk")),
        P("od", None),
        P("od", None),
        P("od", None),
        P("od", None, None, None),
    )
    out_specs = (P(("od", "lk"), None), P(("od", "lk")))
    return jax.shard_map(
        per_device, mesh=mesh, in_specs=in_specs, out_specs=out_specs, check_vma=False
    )
```

time: 160 us -> 160 us (level)
    pallas_call x2 -> x1, Pallas kernels: 128 us -> 128 us  [per_device(): pl.pallas_call(functools.partial(link_kernel, n_od, n_lk, tiles, nb), out...]
where the time goes in v2:
time: 160 us; the launch traced here: 159 us
  Pallas kernels  156 us (98%)
    pallas_call x1, Pallas kernels, per_device(): pl.pallas_call(functools.partial(link_kernel, n_od, n_lk, tiles, nb), out...  128 us
    pallas_call x1, Pallas kernels, per_device(): pl.pallas_call(update_kernel, out_shape=(jax.ShapeDtypeStruct((own_rows,...  28.1 us

profile of v2, /device:TPU:0, one launch (start us, length us, event | category | flops | bytes accessed | tf_op | source)
XLA Modules:
  0.0 159.4 jit_solution(8341814730164654235)
XLA Ops:
  0.6 0.0 copy-start
  0.6 1.5 reshape.31
  2.1 128.2 %links.1.gram_ref = f32[17,8,256]{2,1,0:T(8,128)} custom-call(s32[8,8]{1,0:T(8,128)} %owner_ref.1, s32[8,8]{1,0:T(8,128)} %local_ref.1, s32[8,8]{1,0:T(8,128)} %ecmp_ref.1, f32[64,1,128]{2,1,0:T(1,128)} %bitcast.7, f32[4,128]{1,0:T(4,128)} %bitcast.8, f32[4,128]{1,0:T(4,128)} %bitcast.9, bf16[64,128,256]{2,1,0:T(8,128)(2,1)} %bitcast.6, ...), custom_call_target="tpu_custom_call" | custom-call | tf_op jit(solution)/shard_map/links/pallas_call | solution.py:323
  130.3 0.0 copy-done
  130.3 0.0 copy-start.1
  130.4 0.9 copy-done.1
  131.3 28.1 %update.1 = (f32[4096,256]{1,0:T(8,128)}, f32[8,1,512]{2,1,0:T(1,128)}) custom-call(s32[1]{0:T(128)} %bitcast.start_ref, f32[17,8,256]{2,1,0:T(8,128)S(1)} %copy-done.1, bf16[8192,256]{1,0:T(8,128)(2,1)S(1)} %copy-done), custom_call_target="tpu_custom_call" | custom-call | tf_op jit(solution)/shard_map/update/pallas_call | solution.py:359
Async XLA Ops:
  0.6 129.7 %copy-start = (bf16[8192,256]{1,0:T(8,128)(2,1)S(1)}, bf16[8192,256]{1,0:T(8,128)(2,1)}, u32[]{:S(2)}) copy-start(bf16[8192,256]{1,0:T(8,128)(2,1)} %fac_ref.1) | copy-start | bytes 12582916
  130.3 0.9 copy-start.1

commit v3 on v2

--- a/solution.py
+++ b/solution.py
@@ -108,7 +108,7 @@
         push(send_m.at[peer], got_m, m_send, m_recv, me, peer).start()
         push(send_f.at[peer], got_f, f_send, f_recv, me, peer).start()
 
-    others(serve, True)
+    loop(1, n, lambda step: serve(lax.rem(me + step, n)))
     got_m[me] = jnp.zeros(send_m.shape[1:], jnp.float32)
     for t in range(tiles):
         index = ask_smem[me, 0, t]
@@ -245,7 +245,9 @@
         at, offset = j // 8, j % 8
         here = lane == j
         row = groups[at][offset:offset + 1, :]
-        scaled = jnp.where(here, 1.0, row) / row[:, j:j + 1]
+        pivot = jnp.broadcast_to(row[:, j:j + 1], (1, size))
+        guess = pl.reciprocal(pivot, approx=True)
+        scaled = jnp.where(here, 1.0, row) * (guess * (2.0 - pivot * guess))
         for g in range(at, size // 8):
             if g == at and offset == 7:
                 continue

time: 160 us -> 157 us (0.981)
  Pallas kernels: 156 us -> 154 us
    pallas_call x1, Pallas kernels: 128 us -> 125 us  [per_device(): pl.pallas_call(functools.partial(link_kernel, n_od, n_lk, tiles, nb), out...]
where the time goes in v3:
time: 157 us
  Pallas kernels  154 us (98%)
    pallas_call x1, Pallas kernels, per_device(): pl.pallas_call(functools.partial(link_kernel, n_od, n_lk, tiles, nb), out...  125 us
    pallas_call x1, Pallas kernels, per_device(): pl.pallas_call(update_kernel, out_shape=(jax.ShapeDtypeStruct((own_rows,...  29.6 us

profile of v3, /device:TPU:0, one launch (start us, length us, event | category | flops | bytes accessed | tf_op | source)
XLA Modules:
  0.0 157.1 jit_solution(17823636220559128227)
XLA Ops:
  0.6 0.0 copy-start
  0.6 1.5 reshape.31
  2.1 124.5 %links.1.gram_ref = f32[17,8,256]{2,1,0:T(8,128)} custom-call(s32[8,8]{1,0:T(8,128)} %owner_ref.1, s32[8,8]{1,0:T(8,128)} %local_ref.1, s32[8,8]{1,0:T(8,128)} %ecmp_ref.1, f32[64,1,128]{2,1,0:T(1,128)} %bitcast.7, f32[4,128]{1,0:T(4,128)} %bitcast.8, f32[4,128]{1,0:T(4,128)} %bitcast.9, bf16[64,128,256]{2,1,0:T(8,128)(2,1)} %bitcast.6, ...), custom_call_target="tpu_custom_call" | custom-call | tf_op jit(solution)/shard_map/links/pallas_call | solution.py:325
  126.6 0.0 copy-done
  126.7 0.0 copy-start.1
  126.7 0.9 copy-done.1
  127.6 29.6 %update.1 = (f32[4096,256]{1,0:T(8,128)}, f32[8,1,512]{2,1,0:T(1,128)}) custom-call(s32[1]{0:T(128)} %bitcast.start_ref, f32[17,8,256]{2,1,0:T(8,128)S(1)} %copy-done.1, bf16[8192,256]{1,0:T(8,128)(2,1)S(1)} %copy-done), custom_call_target="tpu_custom_call" | custom-call | tf_op jit(solution)/shard_map/update/pallas_call | solution.py:361
Async XLA Ops:
  0.6 126.0 %copy-start = (bf16[8192,256]{1,0:T(8,128)(2,1)S(1)}, bf16[8192,256]{1,0:T(8,128)(2,1)}, u32[]{:S(2)}) copy-start(bf16[8192,256]{1,0:T(8,128)(2,1)} %fac_ref.1) | copy-start | bytes 12582916
  126.7 0.9 copy-start.1

commit v4 on v2

--- a/solution.py
+++ b/solution.py
@@ -100,15 +100,15 @@
     to_smem.start()
     to_smem.wait()
 
-    def serve(peer):
-        for t in range(tiles):
-            index = ask_smem[peer, 0, t]
-            send_f[peer, t] = fac_ref[index]
-            send_m[peer, t:t + 1] = mean_ref[index]
-        push(send_m.at[peer], got_m, m_send, m_recv, me, peer).start()
-        push(send_f.at[peer], got_f, f_send, f_recv, me, peer).start()
-
-    others(serve, True)
+    def serve(t, peer):
+        index = ask_smem[peer, 0, t]
+        send_f[peer, t] = fac_ref[index]
+        send_m[peer, t:t + 1] = mean_ref[index]
+        push(send_f.at[peer, t], got_f.at[:, t], f_send, f_recv, me, peer).start()
+
+    for t in range(tiles):
+        loop(1, n, lambda step, t=t: serve(t, lax.rem(me + step, n)))
+    others(lambda peer: push(send_m.at[peer], got_m, m_send, m_recv, me, peer).start(), True)
     got_m[me] = jnp.zeros(send_m.shape[1:], jnp.float32)
     for t in range(tiles):
         index = ask_smem[me, 0, t]

time: 160 us -> 157 us (0.981)
  Pallas kernels: 156 us -> 153 us
    pallas_call x1, Pallas kernels: 128 us -> 125 us  [per_device(): pl.pallas_call(functools.partial(link_kernel, n_od, n_lk, tiles, nb), out...]
where the time goes in v4:
time: 157 us; the launch traced here: 156 us
  Pallas kernels  153 us (97%)
    pallas_call x1, Pallas kernels, per_device(): pl.pallas_call(functools.partial(link_kernel, n_od, n_lk, tiles, nb), out...  125 us
    pallas_call x1, Pallas kernels, per_device(): pl.pallas_call(update_kernel, out_shape=(jax.ShapeDtypeStruct((own_rows,...  28.1 us

profile of v4, /device:TPU:0, one launch (start us, length us, event | category | flops | bytes accessed | tf_op | source)
XLA Modules:
  0.0 156.4 jit_solution(474283837767901973)
XLA Ops:
  0.6 0.0 copy-start
  0.6 1.5 reshape.31
  2.1 125.2 %links.1.gram_ref = f32[17,8,256]{2,1,0:T(8,128)} custom-call(s32[8,8]{1,0:T(8,128)} %owner_ref.1, s32[8,8]{1,0:T(8,128)} %local_ref.1, s32[8,8]{1,0:T(8,128)} %ecmp_ref.1, f32[64,1,128]{2,1,0:T(1,128)} %bitcast.7, f32[4,128]{1,0:T(4,128)} %bitcast.8, f32[4,128]{1,0:T(4,128)} %bitcast.9, bf16[64,128,256]{2,1,0:T(8,128)(2,1)} %bitcast.6, ...), custom_call_target="tpu_custom_call" | custom-call | tf_op jit(solution)/shard_map/links/pallas_call | solution.py:323
  127.3 0.0 copy-done
  127.3 0.0 copy-start.1
  127.3 0.9 copy-done.1
  128.2 28.1 %update.1 = (f32[4096,256]{1,0:T(8,128)}, f32[8,1,512]{2,1,0:T(1,128)}) custom-call(s32[1]{0:T(128)} %bitcast.start_ref, f32[17,8,256]{2,1,0:T(8,128)S(1)} %copy-done.1, bf16[8192,256]{1,0:T(8,128)(2,1)S(1)} %copy-done), custom_call_target="tpu_custom_call" | custom-call | tf_op jit(solution)/shard_map/update/pallas_call | solution.py:359
Async XLA Ops:
  0.6 126.7 %copy-start = (bf16[8192,256]{1,0:T(8,128)(2,1)S(1)}, bf16[8192,256]{1,0:T(8,128)(2,1)}, u32[]{:S(2)}) copy-start(bf16[8192,256]{1,0:T(8,128)(2,1)} %fac_ref.1) | copy-start | bytes 12582916
  127.3 0.9 copy-start.1

commit v5 on v4

--- a/solution.py
+++ b/solution.py
@@ -353,7 +353,7 @@
     )
 
     own_rows = factor.shape[0] // n_lk
-    step_rows = min(512, own_rows)
+    step_rows = min(1024, own_rows)
     steps = own_rows // step_rows
     start = (lax.axis_index("lk") * steps).astype(jnp.int32).reshape(1)
     new_factor, correction = pl.pallas_call(

time: 157 us -> 155 us (0.987)
  no operation moved by 1% of the time
where the time goes in v5:
time: 155 us
  Pallas kernels  152 us (98%)
    pallas_call x1, Pallas kernels, per_device(): pl.pallas_call(functools.partial(link_kernel, n_od, n_lk, tiles, nb), out...  125 us
    pallas_call x1, Pallas kernels, per_device(): pl.pallas_call(update_kernel, out_shape=(jax.ShapeDtypeStruct((own_rows,...  26.8 us

profile of v5, /device:TPU:0, one launch (start us, length us, event | category | flops | bytes accessed | tf_op | source)
XLA Modules:
  0.0 155.1 jit_solution(7972213429188220458)
XLA Ops:
  0.6 0.0 copy-start
  0.6 1.5 reshape.31
  2.1 125.2 %links.1.gram_ref = f32[17,8,256]{2,1,0:T(8,128)} custom-call(s32[8,8]{1,0:T(8,128)} %owner_ref.1, s32[8,8]{1,0:T(8,128)} %local_ref.1, s32[8,8]{1,0:T(8,128)} %ecmp_ref.1, f32[64,1,128]{2,1,0:T(1,128)} %bitcast.7, f32[4,128]{1,0:T(4,128)} %bitcast.8, f32[4,128]{1,0:T(4,128)} %bitcast.9, bf16[64,128,256]{2,1,0:T(8,128)(2,1)} %bitcast.6, ...), custom_call_target="tpu_custom_call" | custom-call | tf_op jit(solution)/shard_map/links/pallas_call | solution.py:323
  127.3 0.0 copy-done
  127.3 0.0 copy-start.1
  127.3 0.9 copy-done.1
  128.2 26.8 %update.1 = (f32[4096,256]{1,0:T(8,128)}, f32[4,1,1024]{2,1,0:T(1,128)}) custom-call(s32[1]{0:T(128)} %bitcast.start_ref, f32[17,8,256]{2,1,0:T(8,128)S(1)} %copy-done.1, bf16[8192,256]{1,0:T(8,128)(2,1)S(1)} %copy-done), custom_call_target="tpu_custom_call" | custom-call | tf_op jit(solution)/shard_map/update/pallas_call | solution.py:359
Async XLA Ops:
  0.6 126.7 %copy-start = (bf16[8192,256]{1,0:T(8,128)(2,1)S(1)}, bf16[8192,256]{1,0:T(8,128)(2,1)}, u32[]{:S(2)}) copy-start(bf16[8192,256]{1,0:T(8,128)(2,1)} %fac_ref.1) | copy-start | bytes 12582916
  127.3 0.9 copy-start.1
